TPU v7x, 32 devices: a whole 2x2x4 slice. The times are simulated.
32 devices in a mesh: outer: 2 (over x), sec: 8 (over z, core), tp: 2 (over y).
Axes of the slice: x: 2, y: 2, z: 4, core: 2. Of those that a mesh axis runs over, the one named last changes fastest.
Arguments:
- tile_maps: bfloat16 [32, 12, 12, 3072], P(('outer', 'sec'), None, None, 'tp'), may hold values from -6 to 6
- tile_shape: int32 [32, 2], P(('outer', 'sec')), may hold values from 4 to 12
- conv_kernel: float32 [7, 7, 3072], P(None, None, 'tp'), may hold values from -0.875 to 0.875
- norm_gain: float32 [3072], P('tp'), may hold values from 0.25 to 1.75
- norm_bias: float32 [3072], P('tp'), may hold values from -3 to 3
- projector: bfloat16 [3072, 7168], P('tp', 'sec'), may hold values from -0.109375 to 0.109375
- text_rows: bfloat16 [9216, 7168], P(('outer', 'sec'), 'tp'), may hold values from -6 to 6
- row_order: int32 [16, 576], P(('outer', 'sec')), may hold values from 0 to 575, each once within a row
- seq_gain: float32 [7168], P('tp'), may hold values from 0.25 to 1.75
- cotangent: bfloat16 [9216, 7168], P(('outer', 'sec'), 'tp'), may hold values from -0.2772166 to 0.2772166, as said below
Outputs:
- normed: bfloat16 [9216, 7168], P(('outer', 'sec'), 'tp')
- kernel_delta: float32 [7, 7, 3072], P(None, None, 'tp')
- gain_delta: float32 [3072], P('tp')
- bias_delta: float32 [3072], P('tp')
Inputs may be any that keep to these rules, and one draw needn't show every extreme that they name: `row_order`: each row lists where the visual tokens arriving at that device stand, in arrival order, then the text rows. `tile_shape`: valid rows and columns of each tile, the rest of the map is padding. `cotangent`: gradient of the training loss.
All inputs are finite; a program needn't handle non-finite values.
Results may differ from a plain program's by a relative error of at most 0.0043.
Values may be sent and summed in bfloat16 or wider, within the bound.
A program may use at most 128 MiB of HBM per device.

v0:
```python
import jax
import jax.numpy as jnp
from jax import lax
from jax.sharding import PartitionSpec as P


def shape_mask(tile_shape, grid):
    places = lax.broadcasted_iota(jnp.int32, (1, grid), 1)
    rows_ok = places < tile_shape[:, 0:1]
    cols_ok = places < tile_shape[:, 1:2]
    return (rows_ok[:, :, None] & cols_ok[:, None, :]).astype(jnp.float32)


def on_device(
    tile_maps,
    tile_shape,
    conv_kernel,
    norm_gain,
    norm_bias,
    projector,
    text_rows,
    row_order,
    seq_gain,
    cotangent,
):
    grid = tile_maps.shape[1]
    half_ch = tile_maps.shape[3]
    channels = half_ch * lax.axis_size("tp")
    rows_dev = tile_maps.shape[0] * grid * grid
    width = text_rows.shape[1] * lax.axis_size("tp")
    validity = shape_mask(tile_shape, grid)[..., None]
    masked = tile_maps.astype(jnp.float32) * validity
    padded = jnp.pad(masked, ((0, 0), (3, 3), (3, 3), (0, 0)))
    conv_out = jnp.zeros(masked.shape, jnp.float32)
    for row_off in range(7):
        for col_off in range(7):
            conv_out = (
                conv_out
                + padded[:, row_off : row_off + grid, col_off : col_off + grid, :]
                * conv_kernel[row_off, col_off]
            )
    total_one, total_two = lax.psum(
        (jnp.sum(conv_out, axis=-1), jnp.sum(conv_out * conv_out, axis=-1)), "tp"
    )
    center = (total_one / channels)[..., None]
    inverse = lax.rsqrt((total_two / channels)[..., None] - center * center + 1e-06)
    normal = (conv_out - center) * inverse
    features = (
        (validity * (normal * norm_gain + norm_bias))
        .astype(jnp.bfloat16)
        .reshape(rows_dev, half_ch)
    )
    tp_size = lax.axis_size("tp")
    half_width = text_rows.shape[1]
    mine = lax.axis_index("tp")
    swap = [(i, (i + 1) % tp_size) for i in range(tp_size)]
    gathered = lax.all_gather(projector, "sec", axis=0, tiled=False)
    per_half = gathered.shape[0] // tp_size
    own_weight = lax.dynamic_slice_in_dim(gathered, mine * per_half, per_half, axis=0)
    far_weight = lax.dynamic_slice_in_dim(gathered, (1 - mine) * per_half, per_half, axis=0)
    routed = lax.all_to_all(features, "sec", split_axis=0, concat_axis=0, tiled=True)

    def project(rows, weight):
        return jnp.concatenate(
            [
                jnp.dot(rows, weight[block], preferred_element_type=jnp.float32)
                for block in range(per_half)
            ],
            axis=1,
        )

    sent = project(routed, far_weight).astype(jnp.bfloat16)
    other = lax.ppermute(sent, "tp", swap)
    arrived = (project(routed, own_weight) + other.astype(jnp.float32)).astype(jnp.bfloat16)
    positions = row_order[0, :rows_dev]
    merged = text_rows.at[positions].set(arrived)
    wide = merged.astype(jnp.float32)
    upstream = cotangent.astype(jnp.float32) * seq_gain
    square_sum, along = lax.psum(
        (jnp.sum(wide * wide, axis=-1), jnp.sum(upstream * wide, axis=-1)), "tp"
    )
    inv_rms = lax.rsqrt(square_sum / width + 1e-05)[:, None]
    normed = (wide * inv_rms * seq_gain).astype(jnp.bfloat16)
    grad_seq = inv_rms * upstream - wide * (inv_rms * inv_rms * inv_rms) * along[:, None] / width
    picked = grad_seq[positions].astype(jnp.bfloat16)
    far_picked = lax.ppermute(picked, "tp", swap)

    def project_back(rows, weight):
        step = weight.shape[2]
        total = jnp.zeros((rows.shape[0], half_ch), jnp.float32)
        for block in range(per_half):
            total = total + lax.dot_general(
                rows[:, block * step : (block + 1) * step],
                weight[block],
                (((1,), (1,)), ((), ())),
                preferred_element_type=jnp.float32,
            )
        return total

    back = (project_back(picked, own_weight) + project_back(far_picked, far_weight)).astype(
        jnp.bfloat16
    )
    grad_rows = lax.all_to_all(back, "sec", split_axis=0, concat_axis=0, tiled=True).astype(
        jnp.float32
    )
    masked_grad = grad_rows.reshape(masked.shape) * validity
    scaled = masked_grad * norm_gain
    first_sum, second_sum = lax.psum(
        (jnp.sum(scaled, axis=-1), jnp.sum(scaled * normal, axis=-1)), "tp"
    )
    grad_conv = inverse * (
        scaled - (first_sum / channels)[..., None] - normal * (second_sum / channels)[..., None]
    )
    kernel_rows = []
    for row_off in range(7):
        for col_off in range(7):
            window = padded[:, row_off : row_off + grid, col_off : col_off + grid, :]
            kernel_rows.append(jnp.sum(window * grad_conv, axis=(0, 1, 2)))
    gain_grad = jnp.sum(masked_grad * normal, axis=(0, 1, 2))
    bias_grad = jnp.sum(masked_grad, axis=(0, 1, 2))
    local_delta = jnp.stack(kernel_rows + [gain_grad, bias_grad], axis=0)
    pods = lax.axis_size("outer")
    entries = 51 * channels
    pod_sum = lax.psum(local_delta, "sec")
    norm_sq = lax.psum(jnp.sum(pod_sum * pod_sum), "tp")
    factor = jnp.minimum(1.0, 1.0 / jnp.sqrt(norm_sq / entries + 1e-06))
    average = lax.psum(pod_sum * factor, "outer") / pods
    return (normed, average[:49].reshape(7, 7, half_ch), average[49], average[50])


def solution(mesh):
    in_specs = (
        P(("outer", "sec"), None, None, "tp"),
        P(("outer", "sec"), None),
        P(None, None, "tp"),
        P("tp"),
        P("tp"),
        P("tp", "sec"),
        P(("outer", "sec"), "tp"),
        P(("outer", "sec"), None),
        P("tp"),
        P(("outer", "sec"), "tp"),
    )
    out_specs = (P(("outer", "sec"), "tp"), P(None, None, "tp"), P("tp"), P("tp"))
    return jax.shard_map(
        on_device, mesh=mesh, in_specs=in_specs, out_specs=out_specs, check_vma=False
    )
```

profile of v0, /device:TPU:0, one launch (start us, length us, event | category | flops | bytes accessed | tf_op | source)
XLA Modules:
  0.0 554.4 jit_solution(14218790435124544517)
XLA Ops:
  7.2 4.4 copy.22
  14.4 23.6 %fusion.53 = (f32[2,12,12]{2,1,0:T(8,128)S(1)}, f32[2,12,12]{2,1,0:T(8,128)S(1)}, f32[2,12,12,1536]{3,2,1,0:T(8,128)}) fusion(f32[1536]{0:T(1024)S(1)} %get-tuple-element.110, f32[1536]{0:T(1024)S(1)} %get-tuple-element.111, f32[1536]{0:T(1024)S(1)} %get-tuple-element.64, f32[1536]{0:T(1024)S(1)} %get-tuple-element.65, f32[1536]{0:T(1024)S(1)} %get-tuple-element.66, ...), kind=kLoop, calls=%fused_computation.248 | loop fusion | flops 44236224 | bytes 3842304 | tf_op jit(solution)/shard_map/reduce_sum | solution.py:43
  38.1 9.8 %all-reduce.3 = (f32[2,12,12]{2,1,0:T(8,128)S(1)}, f32[2,12,12]{2,1,0:T(8,128)S(1)}) all-reduce(f32[2,12,12]{2,1,0:T(8,128)S(1)} %get-tuple-element.58, f32[2,12,12]{2,1,0:T(8,128)S(1)} %get-tuple-element.57), channel_id=1, replica_groups=mesh['outer'=2,'sec'=8,'tp'=2] {'tp'}, use_global_device_ids=true, to_apply=%region_3.4 | all-reduce | flops 576 | bytes 4608 | tf_op jit(solution)/shard_map/psum | solution.py:42
  53.1 5.4 all-to-all-start
  58.5 54.2 %all-to-all-done = bf16[8,36,1536]{2,1,0:T(8,128)(2,1)S(1)} async-done(((bf16[8,36,1536]{2,1,0:T(8,128)(2,1)}), bf16[8,36,1536]{2,1,0:T(8,128)(2,1)S(1)}, u32[]{:S(2)}, u32[]{:S(2)}) %all-to-all-start) | async-done | bytes 884768 | tf_op jit(solution)/shard_map/all_to_all | solution.py:61
  113.8 115.7 %all-gather.3.cloned.1.call-done = bf16[12288,896]{1,0:T(8,128)(2,1)} async-done(((bf16[1536,896]{1,0:T(8,128)(2,1)}), bf16[12288,896]{1,0:T(8,128)(2,1)}) %all-gather.3.cloned.1.call-update) | async-done | bytes 22020112 | tf_op jit(solution)/shard_map/all_gather | solution.py:57
  255.8 34.5 %collective-permute-done = bf16[288,3584]{1,0:T(8,128)(2,1)} collective-permute-done((bf16[288,3584]{1,0:T(8,128)(2,1)}, bf16[288,3584]{1,0:T(8,128)(2,1)}, u32[]{:S(2)}, u32[]{:S(2)}) %collective-permute-start) | collective-permute-done | bytes 2064416 | tf_op jit(solution)/shard_map/ppermute | solution.py:73
  293.7 9.2 %scatter_fusion = bf16[576,3584]{1,0:T(8,128)(2,1)} fusion(bf16[576,3584]{1,0:T(8,128)(2,1)} %copy.22, s32[288]{0:T(512)S(1)} %fusion.52, bf16[288,3584]{1,0:T(8,128)(2,1)} %fusion.7), kind=kCustom, calls=%fused_computation.1 | custom fusion | bytes 6194304 | tf_op jit(solution)/shard_map/scatter | solution.py:76
  302.9 5.4 fusion.6
  308.3 5.2 all-reduce.2
  313.5 6.7 %fusion.5 = bf16[576,3584]{1,0:T(8,128)(2,1)} fusion(bf16[576,3584]{1,0:T(8,128)(2,1)} %scatter_fusion, bf16[576,3584]{1,0:T(8,128)(2,1)} %param.19, f32[576]{0:T(1024)S(1)} %get-tuple-element.117, f32[576]{0:T(1024)S(1)} %get-tuple-element.124, f32[3584]{0:T(1024)S(1)} %copy-done.9, f32[576]{0:T(1024)S(1)} %get-tuple-element.125), kind=kLoop, calls=%fused_computation.59 | loop fusion | flops 18579456 | bytes 12407552 | tf_op jit(solution)/shard_map/sub | solution.py:84
  320.2 10.0 %gather_fusion = bf16[288,3584]{1,0:T(8,128)(2,1)} fusion(bf16[576,3584]{1,0:T(8,128)(2,1)} %fusion.5, s32[1024]{0:T(1024)S(1)} %pad_clamp_fusion), kind=kCustom, calls=%fused_computation | custom fusion | bytes 4129920 | tf_op jit(solution)/shard_map/gather | solution.py:85
  343.6 32.0 %collective-permute-done.1 = bf16[288,3584]{1,0:T(8,128)(2,1)S(1)} collective-permute-done((bf16[288,3584]{1,0:T(8,128)(2,1)}, bf16[288,3584]{1,0:T(8,128)(2,1)S(1)}, u32[]{:S(2)}, u32[]{:S(2)}) %collective-permute-start.1) | collective-permute-done | bytes 2064416 | tf_op jit(solution)/shard_map/ppermute | solution.py:86
  388.4 3.9 all-to-all-start.1
  392.4 25.0 %all-to-all-done.1 = bf16[8,36,1536]{2,1,0:T(8,128)(2,1)S(1)} async-done(((bf16[8,36,1536]{2,1,0:T(8,128)(2,1)}), bf16[8,36,1536]{2,1,0:T(8,128)(2,1)S(1)}, u32[]{:S(2)}, u32[]{:S(2)}) %all-to-all-start.1) | async-done | bytes 884768 | tf_op jit(solution)/shard_map/all_to_all | solution.py:103
  422.9 8.5 %all-reduce.1 = (f32[2,12,12]{2,1,0:T(8,128)S(1)}, f32[2,12,12]{2,1,0:T(8,128)S(1)}) all-reduce(f32[2,12,12]{2,1,0:T(8,128)S(1)} %get-tuple-element.5, f32[2,12,12]{2,1,0:T(8,128)S(1)} %reduce_sum.529), channel_id=1, replica_groups=mesh['outer'=2,'sec'=8,'tp'=2] {'tp'}, use_global_device_ids=true, to_apply=%region_12.13 | all-reduce | flops 576 | bytes 4608 | tf_op jit(solution)/shard_map/psum | solution.py:108
  431.4 9.6 %multiply_reduce_fusion.1 = (f32[1536]{0:T(1024)S(1)}, f32[1536]{0:T(1024)S(1)}, f32[1536]{0:T(1024)S(1)}, f32[1536]{0:T(1024)S(1)}, f32[1536]{0:T(1024)S(1)}, /...) fusion(f32[2,12,12,1536]{3,2,1,0:T(8,128)S(1)} %convert_multipl, ...), kind=kLoop, calls=%fused_computation.93 | loop fusion | flops 19436544 | bytes 7200384 | tf_op jit(solution)/shard_map/reduce_sum | solution.py:118
  441.0 5.4 multiply_reduce_fusion.38
  446.4 6.3 %multiply_reduce_fusion.19 = (f32[1536]{0:T(1024)S(1)}, f32[1536]{0:T(1024)S(1)}, f32[1536]{0:T(1024)S(1)}, f32[1536]{0:T(1024)S(1)}, f32[1536]{0:T(1024)S(1)}, ...) fusion(f32[2,12,12,1536]{3,2,1,0:T(8,128)S(1)} %get-tuple-eleme, ...), kind=kLoop, calls=%fused_computation.111 | loop fusion | flops 15897600 | bytes 3649536 | tf_op jit(solution)/shard_map/reduce_sum | solution.py:118
  453.5 4.8 stack.207
  458.4 51.0 %all-reduce.7.cloned.1.call-done = f32[51,1536]{1,0:T(8,128)} async-done(((f32[51,1536]{1,0:T(8,128)}), f32[51,1536]{1,0:T(8,128)}) %all-reduce.7.cloned.1.call-update) | async-done | bytes 313360 | tf_op jit(solution)/shard_map/psum | solution.py:124
  511.0 5.5 %psum.70 = f32[]{:T(128)} all-reduce(f32[]{:T(128)} %multiply_reduce_fusion.54), channel_id=1, replica_groups=mesh['outer'=2,'sec'=8,'tp'=2] {'tp'}, use_global_device_ids=true, to_apply=%region_66.67 | all-reduce | flops 1 | bytes 8 | tf_op jit(solution)/shard_map/psum | solution.py:125
  519.0 5.5 fusion.2
  524.6 20.6 %all-reduce.9.cloned.1.call-done = f32[51,1536]{1,0:T(8,128)} async-done(((f32[51,1536]{1,0:T(8,128)}), f32[51,1536]{1,0:T(8,128)}) %all-reduce.9.cloned.1.call-update) | async-done | bytes 313360 | tf_op jit(solution)/shard_map/psum | solution.py:127
  (130 shorter events, 76.5 us)
Async XLA Ops:
  7.2 222.4 %all-gather.3.cloned.1.call-start = ((), (), s32[]{:S(2)}) async-start(), calls=%async_computation.4 | async-start | bytes 24772608 | tf_op jit(solution)/shard_map/all_gather | solution.py:57
  11.6 0.7 copy-start.11
  11.6 1.0 copy-start.4
  11.6 2.6 copy-start.1
  47.9 0.6 copy-start.5
  47.9 0.6 copy-start.7
  53.1 59.6 %all-to-all-start = ((bf16[8,36,1536]{2,1,0:T(8,128)(2,1)}), bf16[8,36,1536]{2,1,0:T(8,128)(2,1)S(1)}, u32[]{:S(2)}, u32[]{:S(2)}) async-start(bf16[8,36,1536]{2,1,0:T(8,128)(2,1)} %all_to_all.14), calls=%async_computation | async-start | bytes 1966080 | tf_op jit(solution)/shard_map/all_to_all | solution.py:61
  229.5 3.2 copy-start.3
  241.4 3.0 copy-start.12
  242.9 47.4 %collective-permute-start = (bf16[288,3584]{1,0:T(8,128)(2,1)}, bf16[288,3584]{1,0:T(8,128)(2,1)}, u32[]{:S(2)}, u32[]{:S(2)}) collective-permute-start(bf16[288,3584]{1,0:T(8,128)(2,1)} %pad_maximum_fusion), channel_id=1, source_target_pairs={{0,1},{1,0},{2,3},{3,2},{4,5},{5,4},{6,7},{7,6},{8,9},{9,8},{10,11... | collective-permute-start | bytes 6193160 | tf_op jit(solution)/shard_map/ppermute | solution.py:73
  293.7 9.2 %copy-start.9 = (f32[3584]{0:T(1024)S(1)}, f32[3584]{0:T(1024)}, u32[]{:S(2)}) copy-start(f32[3584]{0:T(1024)} %param.18) | copy-start | bytes 43012
  330.3 4.5 copy-start
  330.3 45.3 %collective-permute-start.1 = (bf16[288,3584]{1,0:T(8,128)(2,1)}, bf16[288,3584]{1,0:T(8,128)(2,1)S(1)}, u32[]{:S(2)}, u32[]{:S(2)}) collective-permute-start(bf16[288,3584]{1,0:T(8,128)(2,1)} %gather_fusion), channel_id=1, source_target_pairs={{0,1},{1,0},{2,3},{3,2},{4,5},{5,4},{6,7},{7,6},{8,9},{9,8},{10,11... | collective-permute-start | bytes 6193160 | tf_op jit(solution)/shard_map/ppermute | solution.py:86
  388.4 30.5 %copy-start.6 = (f32[2,12,12]{2,1,0:T(8,128)S(1)}, f32[2,12,12]{2,1,0:T(8,128)}, u32[]{:S(2)}) copy-start(f32[2,12,12]{2,1,0:T(8,128)} %copy-done.5) | copy-start | bytes 3460
  388.4 30.5 %copy-start.8 = (f32[2,12,12]{2,1,0:T(8,128)S(1)}, f32[2,12,12]{2,1,0:T(8,128)}, u32[]{:S(2)}) copy-start(f32[2,12,12]{2,1,0:T(8,128)} %copy-done.7) | copy-start | bytes 3460
  388.4 30.5 %copy-start.10 = (f32[1536]{0:T(1024)S(1)}, f32[1536]{0:T(1024)}, u32[]{:S(2)}) copy-start(f32[1536]{0:T(1024)} %param.13) | copy-start | bytes 18436
  388.4 29.0 %all-to-all-start.1 = ((bf16[8,36,1536]{2,1,0:T(8,128)(2,1)}), bf16[8,36,1536]{2,1,0:T(8,128)(2,1)S(1)}, u32[]{:S(2)}, u32[]{:S(2)}) async-start(bf16[8,36,1536]{2,1,0:T(8,128)(2,1)} %all_to_all.17), calls=%async_computation.1 | async-start | bytes 1966080 | tf_op jit(solution)/shard_map/all_to_all | solution.py:103
  392.3 117.0 %all-reduce.7.cloned.1.call-start = ((), (), s32[]{:S(2)}) async-start(), calls=%async_computation.2 | async-start | bytes 688128 | tf_op jit(solution)/shard_map/psum | solution.py:124
  431.3 9.6 %copy-start.2 = (bf16[2,12,12,1536]{3,0,2,1:T(2,128)(2,1)S(1)}, bf16[2,12,12,1536]{3,0,2,1:T(2,128)(2,1)}, u32[]{:S(2)}) copy-start(bf16[2,12,12,1536]{3,0,2,1:T(2,128)(2,1)} %param.10) | copy-start | bytes 2654212
  458.3 86.9 %all-reduce.9.cloned.1.call-start = ((), (), s32[]{:S(2)}) async-start(), calls=%async_computation.3 | async-start | bytes 688128 | tf_op jit(solution)/shard_map/psum | solution.py:127
Sparse Core Ops, SparseCore 0:
  11.8 217.7 all-gather.2
  458.4 50.8 all-reduce.6
  519.2 25.9 all-reduce.8
where the time goes:
time: 561 us; the launch traced here: 554 us
  waiting for transfers between devices  333 us (59%)
  other arithmetic  79.7 us (14%)
  matrix products  46.6 us (8%)
  local copies, waits for them, and re-layouts  38.2 us (7%)
  blocking collectives  29 us (5%)
  between operations  15.4 us (3%)
  starting transfers between devices  12.3 us (2%)
    all_gather x1, waiting for transfers between devices, on_device(): gathered = lax.all_gather(projector, 'sec', axis=0, tiled=False)  116 us
    all_to_all x1, waiting for transfers between devices, on_device(): lax.all_to_all(features, 'sec', split_axis=0, concat_axis=0, tiled=True)  54.2 us
    psum x1, waiting for transfers between devices, on_device(): pod_sum = lax.psum(local_delta, 'sec')  51 us
    ppermute x1, waiting for transfers between devices, on_device(): other = lax.ppermute(sent, 'tp', swap)  34.5 us
    ppermute x1, waiting for transfers between devices, on_device(): far_picked = lax.ppermute(picked, 'tp', swap)  32 us
    all_to_all x1, waiting for transfers between devices, on_device(): lax.all_to_all(back, 'sec', split_axis=0, concat_axis=0, tiled=True)  25 us
    reduce_sum x1, other arithmetic, on_device(): jnp.sum(conv_out, axis=-1)  23.6 us
    dot_general x8, matrix products, project_back(): lax.dot_general(rows[:, block * step:(block + 1) * step], weight[block],...  23.4 us
  transfers between devices with their start and end apart: 7, of which 7 were waited for; matrix products, arithmetic and copies ran while one was open for 10% of the time, Pallas kernels for 0%

commit v1 on v0

--- a/solution.py
+++ b/solution.py
@@ -23,6 +23,23 @@
     seq_gain,
     cotangent,
 ):
+
+    def state_signs(inputs):
+        y2 = lax.axis_size("sec")
+        arr_next = lax.axis_index("sec")
+        spare, before = (y2, arr_next)
+        shaped = inputs.shape[0] // spare
+        a_now = jnp.roll(inputs, shift=-before * shaped, axis=0)
+        v_next = lax.slice_in_dim(a_now, 0, shaped, axis=0)
+        parts_seen = [v_next]
+        for t in range(1, spare):
+            arr_now = lax.slice_in_dim(a_now, t * shaped, (t + 1) * shaped, axis=0)
+            parts_seen.append(
+                lax.ppermute(arr_now, "sec", [(w, (w + t) % spare) for w in range(spare)])
+            )
+        wide_out = jnp.concatenate(parts_seen[::-1], axis=0)
+        return jnp.roll(wide_out, (before + 1) * parts_seen[0].shape[0], axis=0)
+
     grid = tile_maps.shape[1]
     half_ch = tile_maps.shape[3]
     channels = half_ch * lax.axis_size("tp")
@@ -100,9 +117,7 @@
     back = (project_back(picked, own_weight) + project_back(far_picked, far_weight)).astype(
         jnp.bfloat16
     )
-    grad_rows = lax.all_to_all(back, "sec", split_axis=0, concat_axis=0, tiled=True).astype(
-        jnp.float32
-    )
+    grad_rows = state_signs(back).astype(jnp.float32)
     masked_grad = grad_rows.reshape(masked.shape) * validity
     scaled = masked_grad * norm_gain
     first_sum, second_sum = lax.psum(

time: 561 us -> 568 us (1.012)
  local copies, waits for them, and re-layouts: 38.2 us -> 47.2 us
  waiting for transfers between devices: 333 us -> 327 us
    all_to_all x1 -> x0, waiting for transfers between devices: 25 us -> none  [on_device(): lax.all_to_all(back, 'sec', split_axis=0, concat_axis=0, tiled=True)]
    ppermute x0 -> x7, waiting for transfers between devices: none -> 13.2 us  [state_signs(): lax.ppermute(arr_now, 'sec', [(w, (w + t) % spare) for w in range(spare)])]
    concatenate x0 -> x1, local copies, waits for them, and re-layouts: none -> 6.06 us  [state_signs(): wide_out = jnp.concatenate(parts_seen[::-1], axis=0)]
  transfers between devices with their start and end apart: 7 -> 13, of which waited for: 7 -> 10; matrix products, arithmetic and copies ran while one was open for 10% -> 10% of each run, Pallas kernels for 0% -> 0%
where the time goes in v1:
time: 568 us; the launch traced here: 562 us
  waiting for transfers between devices  327 us (58%)
  other arithmetic  82.5 us (15%)
  matrix products  47.5 us (8%)
  local copies, waits for them, and re-layouts  47.2 us (8%)
  blocking collectives  28.7 us (5%)
  between operations  15.5 us (3%)
  starting transfers between devices  13 us (2%)
    all_gather x1, waiting for transfers between devices, on_device(): gathered = lax.all_gather(projector, 'sec', axis=0, tiled=False)  116 us
    psum x1, waiting for transfers between devices, on_device(): pod_sum = lax.psum(local_delta, 'sec')  56.6 us
    all_to_all x1, waiting for transfers between devices, on_device(): lax.all_to_all(features, 'sec', split_axis=0, concat_axis=0, tiled=True)  54.4 us
    ppermute x1, waiting for transfers between devices, on_device(): other = lax.ppermute(sent, 'tp', swap)  34.5 us
    ppermute x1, waiting for transfers between devices, on_device(): far_picked = lax.ppermute(picked, 'tp', swap)  32 us
    dot_general x8, matrix products, project_back(): lax.dot_general(rows[:, block * step:(block + 1) * step], weight[block],...  24.3 us
    reduce_sum x1, other arithmetic, on_device(): jnp.sum(conv_out, axis=-1)  23.6 us
    dot_general x8, matrix products, project(): jnp.dot(rows, weight[block], preferred_element_type=jnp.float32)  23.2 us
  transfers between devices with their start and end apart: 13, of which 10 were waited for; matrix products, arithmetic and copies ran while one was open for 10% of the time, Pallas kernels for 0%

profile of v1, /device:TPU:0, one launch (start us, length us, event | category | flops | bytes accessed | tf_op | source)
XLA Modules:
  0.0 561.5 jit_solution(13421777247876512216)
XLA Ops:
  7.2 4.4 copy.23
  14.4 23.6 %fusion.56 = (f32[2,12,12]{2,1,0:T(8,128)S(1)}, f32[2,12,12]{2,1,0:T(8,128)S(1)}, f32[2,12,12,1536]{3,2,1,0:T(8,128)}) fusion(f32[1536]{0:T(1024)S(1)} %get-tuple-element.111, f32[1536]{0:T(1024)S(1)} %get-tuple-element.112, f32[1536]{0:T(1024)S(1)} %get-tuple-element.65, f32[1536]{0:T(1024)S(1)} %get-tuple-element.66, f32[1536]{0:T(1024)S(1)} %get-tuple-element.67, ...), kind=kLoop, calls=%fused_computation.255 | loop fusion | flops 44236224 | bytes 3842304 | tf_op jit(solution)/shard_map/reduce_sum | solution.py:60
  38.1 9.8 %all-reduce.3 = (f32[2,12,12]{2,1,0:T(8,128)S(1)}, f32[2,12,12]{2,1,0:T(8,128)S(1)}) all-reduce(f32[2,12,12]{2,1,0:T(8,128)S(1)} %get-tuple-element.59, f32[2,12,12]{2,1,0:T(8,128)S(1)} %get-tuple-element.58), channel_id=1, replica_groups=mesh['outer'=2,'sec'=8,'tp'=2] {'tp'}, use_global_device_ids=true, to_apply=%region_3.4 | all-reduce | flops 576 | bytes 4608 | tf_op jit(solution)/shard_map/psum | solution.py:59
  53.1 4.9 all-to-all-start
  58.3 54.4 %all-to-all-done = bf16[8,36,1536]{2,1,0:T(8,128)(2,1)S(1)} async-done(((bf16[8,36,1536]{2,1,0:T(8,128)(2,1)}), bf16[8,36,1536]{2,1,0:T(8,128)(2,1)S(1)}, u32[]{:S(2)}, u32[]{:S(2)}) %all-to-all-start) | async-done | bytes 884768 | tf_op jit(solution)/shard_map/all_to_all | solution.py:78
  113.8 115.7 %all-gather.3.cloned.1.call-done = bf16[12288,896]{1,0:T(8,128)(2,1)} async-done(((bf16[1536,896]{1,0:T(8,128)(2,1)}), bf16[12288,896]{1,0:T(8,128)(2,1)}) %all-gather.3.cloned.1.call-update) | async-done | bytes 22020112 | tf_op jit(solution)/shard_map/all_gather | solution.py:74
  255.8 34.5 %collective-permute-done = bf16[288,3584]{1,0:T(8,128)(2,1)} collective-permute-done((bf16[288,3584]{1,0:T(8,128)(2,1)}, bf16[288,3584]{1,0:T(8,128)(2,1)}, u32[]{:S(2)}, u32[]{:S(2)}) %collective-permute-start) | collective-permute-done | bytes 2064416 | tf_op jit(solution)/shard_map/ppermute | solution.py:90
  293.7 9.7 %scatter_fusion = bf16[576,3584]{1,0:T(8,128)(2,1)} fusion(bf16[576,3584]{1,0:T(8,128)(2,1)} %copy.23, s32[288]{0:T(512)S(1)} %fusion.55, bf16[288,3584]{1,0:T(8,128)(2,1)} %fusion.7), kind=kCustom, calls=%fused_computation.1 | custom fusion | bytes 6194304 | tf_op jit(solution)/shard_map/scatter | solution.py:93
  303.4 5.4 fusion.6
  308.9 5.0 all-reduce.2
  313.9 6.7 %fusion.5 = bf16[576,3584]{1,0:T(8,128)(2,1)} fusion(bf16[576,3584]{1,0:T(8,128)(2,1)} %scatter_fusion, bf16[576,3584]{1,0:T(8,128)(2,1)} %param.21, f32[576]{0:T(1024)S(1)} %get-tuple-element.118, f32[576]{0:T(1024)S(1)} %get-tuple-element.134, f32[3584]{0:T(1024)S(1)} %copy-done.9, f32[576]{0:T(1024)S(1)} %get-tuple-element.135), kind=kLoop, calls=%fused_computation.59 | loop fusion | flops 18579456 | bytes 12407552 | tf_op jit(solution)/shard_map/sub | solution.py:101
  320.6 10.2 %gather_fusion = bf16[288,3584]{1,0:T(8,128)(2,1)} fusion(bf16[576,3584]{1,0:T(8,128)(2,1)} %fusion.5, s32[1024]{0:T(1024)S(1)} %pad_clamp_fusion), kind=kCustom, calls=%fused_computation | custom fusion | bytes 4129920 | tf_op jit(solution)/shard_map/gather | solution.py:102
  344.3 32.0 %collective-permute-done.1 = bf16[288,3584]{1,0:T(8,128)(2,1)} collective-permute-done((bf16[288,3584]{1,0:T(8,128)(2,1)}, bf16[288,3584]{1,0:T(8,128)(2,1)}, u32[]{:S(2)}, u32[]{:S(2)}) %collective-permute-start.1) | collective-permute-done | bytes 2064416 | tf_op jit(solution)/shard_map/ppermute | solution.py:103
  399.5 9.0 %collective-permute-done.6 = bf16[36,1536]{1,0:T(8,128)(2,1)S(1)} collective-permute-done((bf16[36,1536]{1,0:T(8,128)(2,1)}, bf16[36,1536]{1,0:T(8,128)(2,1)S(1)}, u32[]{:S(2)}, u32[]{:S(2)}) %collective-permute-start.6) | collective-permute-done | bytes 110624 | tf_op jit(solution)/shard_map/ppermute | solution.py:38
  410.0 6.1 %concatenate.15 = bf16[288,1536]{1,0:T(8,128)(2,1)S(1)} concatenate(bf16[36,1536]{1,0:T(8,128)(2,1)} %copy-done.15, bf16[36,1536]{1,0:T(8,128)(2,1)} %copy-done.14, bf16[36,1536]{1,0:T(8,128)(2,1)} %copy-done.13, bf16[36,1536]{1,0:T(8,128)(2,1)} %copy-done.12, bf16[36,1536]{1,0:T(8,128)(2,1)} %copy-done.11, bf16[36,1536]{1,0:T(8,128)(2,1)} %collective-permute-done.7, ...), dimensions={0} | concatenate | bytes 1769472 | tf_op jit(solution)/shard_map/concatenate | solution.py:40
  424.4 8.3 %all-reduce.1 = (f32[2,12,12]{2,1,0:T(8,128)S(1)}, f32[2,12,12]{2,1,0:T(8,128)S(1)}) all-reduce(f32[2,12,12]{2,1,0:T(8,128)S(1)} %get-tuple-element.6, f32[2,12,12]{2,1,0:T(8,128)S(1)} %reduce_sum.529), channel_id=1, replica_groups=mesh['outer'=2,'sec'=8,'tp'=2] {'tp'}, use_global_device_ids=true, to_apply=%region_12.14 | all-reduce | flops 576 | bytes 4608 | tf_op jit(solution)/shard_map/psum | solution.py:123
  432.7 9.8 %multiply_reduce_fusion.1 = (f32[1536]{0:T(1024)S(1)}, f32[1536]{0:T(1024)S(1)}, f32[1536]{0:T(1024)S(1)}, f32[1536]{0:T(1024)S(1)}, f32[1536]{0:T(1024)S(1)}, /...) fusion(f32[2,12,12,1536]{3,2,1,0:T(8,128)S(1)} %convert_multipl, ...), kind=kLoop, calls=%fused_computation.93 | loop fusion | flops 19436544 | bytes 7200384 | tf_op jit(solution)/shard_map/reduce_sum | solution.py:133
  442.5 5.4 multiply_reduce_fusion.38
  448.0 6.3 %multiply_reduce_fusion.19 = (f32[1536]{0:T(1024)S(1)}, f32[1536]{0:T(1024)S(1)}, f32[1536]{0:T(1024)S(1)}, f32[1536]{0:T(1024)S(1)}, f32[1536]{0:T(1024)S(1)}, ...) fusion(f32[2,12,12,1536]{3,2,1,0:T(8,128)S(1)} %get-tuple-eleme, ...), kind=kLoop, calls=%fused_computation.111 | loop fusion | flops 15897600 | bytes 3649536 | tf_op jit(solution)/shard_map/reduce_sum | solution.py:133
  455.0 4.8 stack.207
  459.9 56.6 %all-reduce.7.cloned.1.call-done = f32[51,1536]{1,0:T(8,128)} async-done(((f32[51,1536]{1,0:T(8,128)}), f32[51,1536]{1,0:T(8,128)}) %all-reduce.7.cloned.1.call-update) | async-done | bytes 313360 | tf_op jit(solution)/shard_map/psum | solution.py:139
  518.2 5.5 psum.70
  526.2 5.5 fusion.2
  531.7 20.6 %all-reduce.9.cloned.1.call-done = f32[51,1536]{1,0:T(8,128)} async-done(((f32[51,1536]{1,0:T(8,128)}), f32[51,1536]{1,0:T(8,128)}) %all-reduce.9.cloned.1.call-update) | async-done | bytes 313360 | tf_op jit(solution)/shard_map/psum | solution.py:142
  (154 shorter events, 91.6 us)
Async XLA Ops:
  7.2 222.4 %all-gather.3.cloned.1.call-start = ((), (), s32[]{:S(2)}) async-start(), calls=%async_computation.3 | async-start | bytes 24772608 | tf_op jit(solution)/shard_map/all_gather | solution.py:74
  11.6 1.0 copy-start.4
  11.6 2.6 copy-start.1
  53.1 59.6 %all-to-all-start = ((bf16[8,36,1536]{2,1,0:T(8,128)(2,1)}), bf16[8,36,1536]{2,1,0:T(8,128)(2,1)S(1)}, u32[]{:S(2)}, u32[]{:S(2)}) async-start(bf16[8,36,1536]{2,1,0:T(8,128)(2,1)} %all_to_all.8), calls=%async_computation | async-start | bytes 1966080 | tf_op jit(solution)/shard_map/all_to_all | solution.py:78
  58.0 458.6 %all-reduce.7.cloned.1.call-start = ((), (), s32[]{:S(2)}) async-start(), calls=%async_computation.1 | async-start | bytes 688128 | tf_op jit(solution)/shard_map/psum | solution.py:139
  229.5 3.2 copy-start.3
  241.4 3.0 copy-start.17
  242.9 47.4 %collective-permute-start = (bf16[288,3584]{1,0:T(8,128)(2,1)}, bf16[288,3584]{1,0:T(8,128)(2,1)}, u32[]{:S(2)}, u32[]{:S(2)}) collective-permute-start(bf16[288,3584]{1,0:T(8,128)(2,1)} %pad_maximum_fusion), channel_id=1, source_target_pairs={{0,1},{1,0},{2,3},{3,2},{4,5},{5,4},{6,7},{7,6},{8,9},{9,8},{10,11... | collective-permute-start | bytes 6193160 | tf_op jit(solution)/shard_map/ppermute | solution.py:90
  293.7 9.7 %copy-start.9 = (f32[3584]{0:T(1024)S(1)}, f32[3584]{0:T(1024)}, u32[]{:S(2)}) copy-start(f32[3584]{0:T(1024)} %param.20) | copy-start | bytes 43012
  330.8 45.5 %collective-permute-start.1 = (bf16[288,3584]{1,0:T(8,128)(2,1)}, bf16[288,3584]{1,0:T(8,128)(2,1)}, u32[]{:S(2)}, u32[]{:S(2)}) collective-permute-start(bf16[288,3584]{1,0:T(8,128)(2,1)} %gather_fusion), channel_id=1, source_target_pairs={{0,1},{1,0},{2,3},{3,2},{4,5},{5,4},{6,7},{7,6},{8,9},{9,8},{10,11... | collective-permute-start | bytes 6193160 | tf_op jit(solution)/shard_map/ppermute | solution.py:103
  332.4 3.2 copy-start
  389.7 26.3 %copy-start.10 = (f32[1536]{0:T(1024)S(1)}, f32[1536]{0:T(1024)}, u32[]{:S(2)}) copy-start(f32[1536]{0:T(1024)} %param.15) | copy-start | bytes 18436
  390.6 7.0 %collective-permute-start.8 = (bf16[36,1536]{1,0:T(8,128)(2,1)S(1)}, bf16[36,1536]{1,0:T(8,128)(2,1)S(1)}, u32[]{:S(2)}, u32[]{:S(2)}) collective-permute-start(bf16[36,1536]{1,0:T(8,128)(2,1)S(1)} %get-tuple-element.125), channel_id=1, source_target_pairs={{0,2},{2,4},{4,6},{6,8},{8,10},{10,12},{12,14},{14,0},{1,3},{3,5},... | collective-permute-start | bytes 331784 | tf_op jit(solution)/shard_map/ppermute | solution.py:38
  390.6 8.2 %collective-permute-start.7 = (bf16[36,1536]{1,0:T(8,128)(2,1)S(1)}, bf16[36,1536]{1,0:T(8,128)(2,1)}, u32[]{:S(2)}, u32[]{:S(2)}) collective-permute-start(bf16[36,1536]{1,0:T(8,128)(2,1)S(1)} %get-tuple-element.126), channel_id=1, source_target_pairs={{0,4},{2,6},{4,8},{6,10},{8,12},{10,14},{12,0},{14,2},{1,5},{3,7},... | collective-permute-start | bytes 331784 | tf_op jit(solution)/shard_map/ppermute | solution.py:38
  390.6 17.9 %collective-permute-start.6 = (bf16[36,1536]{1,0:T(8,128)(2,1)}, bf16[36,1536]{1,0:T(8,128)(2,1)S(1)}, u32[]{:S(2)}, u32[]{:S(2)}) collective-permute-start(bf16[36,1536]{1,0:T(8,128)(2,1)} %get-tuple-element.127), channel_id=1, source_target_pairs={{0,6},{2,8},{4,10},{6,12},{8,14},{10,0},{12,2},{14,4},{1,7},{3,9},... | collective-permute-start | bytes 331784 | tf_op jit(solution)/shard_map/ppermute | solution.py:38
  391.5 17.1 %collective-permute-start.5 = (bf16[36,1536]{1,0:T(8,128)(2,1)}, bf16[36,1536]{1,0:T(8,128)(2,1)S(1)}, u32[]{:S(2)}, u32[]{:S(2)}) collective-permute-start(bf16[36,1536]{1,0:T(8,128)(2,1)} %get-tuple-element.128), channel_id=1, source_target_pairs={{0,8},{2,10},{4,12},{6,14},{8,0},{10,2},{12,4},{14,6},{1,9},{3,11}... | collective-permute-start | bytes 331784 | tf_op jit(solution)/shard_map/ppermute | solution.py:38
  394.7 13.9 %collective-permute-start.4 = (bf16[36,1536]{1,0:T(8,128)(2,1)}, bf16[36,1536]{1,0:T(8,128)(2,1)S(1)}, u32[]{:S(2)}, u32[]{:S(2)}) collective-permute-start(bf16[36,1536]{1,0:T(8,128)(2,1)} %get-tuple-element.129), channel_id=1, source_target_pairs={{0,10},{2,12},{4,14},{6,0},{8,2},{10,4},{12,6},{14,8},{1,11},{3,13... | collective-permute-start | bytes 331784 | tf_op jit(solution)/shard_map/ppermute | solution.py:38
  397.5 11.1 %collective-permute-start.3 = (bf16[36,1536]{1,0:T(8,128)(2,1)S(1)}, bf16[36,1536]{1,0:T(8,128)(2,1)S(1)}, u32[]{:S(2)}, u32[]{:S(2)}) collective-permute-start(bf16[36,1536]{1,0:T(8,128)(2,1)S(1)} %get-tuple-element.130), channel_id=1, source_target_pairs={{0,12},{2,14},{4,0},{6,2},{8,4},{10,6},{12,8},{14,10},{1,13},{3,15... | collective-permute-start | bytes 331784 | tf_op jit(solution)/shard_map/ppermute | solution.py:38
  398.8 9.8 %collective-permute-start.2 = (bf16[36,1536]{1,0:T(8,128)(2,1)S(1)}, bf16[36,1536]{1,0:T(8,128)(2,1)S(1)}, u32[]{:S(2)}, u32[]{:S(2)}) collective-permute-start(bf16[36,1536]{1,0:T(8,128)(2,1)S(1)} %get-tuple-element.131), channel_id=1, source_target_pairs={{0,14},{2,0},{4,2},{6,4},{8,6},{10,8},{12,10},{14,12},{1,15},{3,1}... | collective-permute-start | bytes 331784 | tf_op jit(solution)/shard_map/ppermute | solution.py:38
  408.6 0.7 copy-start.14
  418.1 2.9 copy-start.6
  418.1 2.9 copy-start.8
  432.7 9.8 %copy-start.2 = (bf16[2,12,12,1536]{3,0,2,1:T(2,128)(2,1)S(1)}, bf16[2,12,12,1536]{3,0,2,1:T(2,128)(2,1)}, u32[]{:S(2)}) copy-start(bf16[2,12,12,1536]{3,0,2,1:T(2,128)(2,1)} %param.12) | copy-start | bytes 2654212
  459.9 92.5 %all-reduce.9.cloned.1.call-start = ((), (), s32[]{:S(2)}) async-start(), calls=%async_computation.2 | async-start | bytes 688128 | tf_op jit(solution)/shard_map/psum | solution.py:142
  (7 other events, 4.5 us)
Sparse Core Ops, SparseCore 0:
  11.8 217.7 all-gather.2
  460.0 56.5 all-reduce.6
  526.3 25.9 all-reduce.8
